TPU v7x, 128 devices: a whole 4x4x4 slice. The times are simulated.
128 devices in a mesh: wide: 32 (over z, y, core), narrow: 4 (over x).
Axes of the slice: x: 4, y: 4, z: 4, core: 2. Of those that a mesh axis runs over, the one named last changes fastest.
Arguments:
- embeddings: float32 [16384, 1024], P(('wide', 'narrow')), may hold values from -6 to 6
- cluster: int32 [16384], P(('wide', 'narrow')), may hold values from 0 to 63, as said below
- order: int32 [16384], P(('wide', 'narrow')), may hold values from 0 to 511
Outputs:
- best_similarity: float32 [16384], P(('wide', 'narrow'))
Inputs may be any that keep to these rules, and one draw needn't show every extreme that they name: Documents of one cluster have distinct order values. For every k, at most 8 documents of one device lie in clusters k * 2 to k * 2 + 1, and on every device exactly 8 for some k.
All inputs are finite; a program needn't handle non-finite values.
Results may differ from a plain program's by a relative error of at most 0.0013.
Values may be sent and summed in bfloat16 or wider, within the bound.
No kernel may reach another device: no remote copies, remote signals or barrier semaphores. Data moves between devices by JAX's collectives and lax.ppermute only.
A program may use at most 64 MiB of HBM per device.

v0:
```python
import jax
import jax.numpy as jnp
from jax import lax
from jax.experimental import pallas as pl
from jax.experimental.pallas import tpu as pltpu
from jax.sharding import Mesh, PartitionSpec as P

CLUSTERS = 64
SLOTS = 8
CAP = 512
LANES = 128
CORES = 2
epsilon = 1e-06

VMEM = 32 * 1024 * 1024
NT = (((1,), (1,)), ((), ()))


def iota(shape, axis):
    return lax.broadcasted_iota(jnp.int32, shape, axis)


def as_bf16(mask):
    return jnp.where(mask, 1.0, 0.0).astype(jnp.bfloat16)


def pack_kernel(rows_hbm, cluster_hbm, order_hbm, out_ref, where_ref, rows_ref, ids_ref, sems):
    docs, width = rows_ref.shape
    slots = out_ref.shape[0]
    cluster_copy = pltpu.make_async_copy(cluster_hbm, ids_ref.at[0], sems.at[0])
    order_copy = pltpu.make_async_copy(order_hbm, ids_ref.at[1], sems.at[1])
    rows_copy = pltpu.make_async_copy(rows_hbm, rows_ref, sems.at[2])
    cluster_copy.start()
    order_copy.start()
    rows_copy.start()
    before = as_bf16(iota((docs, docs), 0) < iota((docs, docs), 1))
    line = iota((LANES, docs), 0)
    slot = iota((slots, docs), 0)
    cluster_copy.wait()
    order_copy.wait()
    cluster = ids_ref[0]
    member = iota((CLUSTERS, docs), 0) == cluster
    count = jnp.dot(as_bf16(member), before, preferred_element_type=jnp.float32)
    position = jnp.sum(jnp.where(member, count, 0.0), axis=0, keepdims=True).astype(jnp.int32)
    chip = lax.axis_index("zy") * lax.axis_size("x") + lax.axis_index("x")
    where_ref[0:1] = cluster
    where_ref[1:2] = chip % (LANES // SLOTS) * SLOTS + position
    place = as_bf16(slot == cluster * SLOTS + position)
    rank = ids_ref[1] - CAP
    high = (rank >> 4).astype(jnp.float32)
    low = (rank & 15).astype(jnp.float32)
    ranks = jnp.where(line == 0, high, jnp.where(line == 1, low, 0.0)).astype(jnp.bfloat16)
    out_ref[:, width:] = lax.dot_general(
        place, ranks, NT, preferred_element_type=jnp.float32
    ).astype(jnp.bfloat16)
    rows_copy.wait()
    rows = rows_ref[...]
    squares = jnp.sum(rows * rows, axis=1, keepdims=True)
    unit = (rows * lax.rsqrt(squares + epsilon)).astype(jnp.bfloat16)
    out_ref[:, :width] = jnp.dot(place, unit, preferred_element_type=jnp.float32).astype(
        jnp.bfloat16
    )


def rank_weights(shape, axis):
    at = iota(shape, axis)
    return jnp.where(at == 0, 16.0, jnp.where(at == 1, 1.0, 0.0)).astype(jnp.bfloat16)


def best_of(keys_ref, queries_ref, rank_ref, width, first):
    keys = keys_ref.shape[0]
    key_rank = jnp.dot(
        keys_ref[:, width:],
        rank_weights((LANES, LANES), 0),
        preferred_element_type=jnp.float32,
    )
    step = 2 * LANES
    best = []
    for at in range(0, queries_ref.shape[1], step):
        similar = jnp.dot(
            keys_ref[:, :width],
            queries_ref[:, at : at + step],
            preferred_element_type=jnp.float32,
        )
        for lane in range(0, step, LANES):
            allowed = key_rank < rank_ref[0:1, at + lane : at + lane + LANES]
            value = jnp.where(allowed, similar[:, lane : lane + LANES], -1.0)
            value = jnp.max(value.reshape(keys // 8, 8, LANES), axis=0)
            best.append(jnp.maximum(value, first[:, at + lane : at + lane + LANES]))
    return best


def own_kernel(own_ref, queries_ref, rank_ref, best_ref):
    slots, width = own_ref.shape[0], own_ref.shape[1] - LANES
    queries_ref[...] = own_ref[:, :width].T
    rank_ref[...] = lax.dot_general(
        rank_weights((8, LANES), 1), own_ref[:, width:], NT, preferred_element_type=jnp.float32
    )
    first = jnp.full((8, slots), -1.0, jnp.float32)
    for at, best in enumerate(best_of(own_ref, queries_ref, rank_ref, width, first)):
        best_ref[:, at * LANES : (at + 1) * LANES] = best


def other_kernel(other_ref, queries_ref, rank_ref, first_ref, out_ref):
    width = queries_ref.shape[0]
    lines = LANES // SLOTS
    for at, best in enumerate(best_of(other_ref, queries_ref, rank_ref, width, first_ref[...])):
        best = jnp.max(best, axis=0, keepdims=True)
        out_ref[at * lines : (at + 1) * lines] = jnp.broadcast_to(best, (lines, LANES))


def unpack_kernel(best_ref, where_ref, out_ref):
    docs = where_ref.shape[1]
    best = jnp.concatenate([best_ref[...], jnp.zeros((LANES - CLUSTERS, LANES), jnp.float32)])
    cluster = jnp.broadcast_to(where_ref[0:1], (LANES, docs))
    by_cluster = jnp.take_along_axis(best.T, cluster, axis=1)
    wanted = iota((LANES, docs), 0) == where_ref[1:2]
    out_ref[...] = jnp.sum(jnp.where(wanted, by_cluster, 0.0), axis=0, keepdims=True)


def call(kernel, out_shape, flops, moved, **more):
    return pl.pallas_call(
        kernel,
        out_shape=out_shape,
        compiler_params=pltpu.CompilerParams(vmem_limit_bytes=VMEM),
        cost_estimate=pl.CostEstimate(flops=flops, bytes_accessed=moved, transcendentals=0),
        **more,
    )


def in_hbm(x):
    return pltpu.with_memory_space_constraint(x, pltpu.HBM)


def per_device(embeddings, cluster, order):
    docs, width = embeddings.shape
    slots = CLUSTERS * SLOTS
    wide = width + LANES
    shape = jax.ShapeDtypeStruct
    f32, bf16, i32 = jnp.float32, jnp.bfloat16, jnp.int32
    packed, where = call(
        pack_kernel,
        (shape((slots, wide), bf16), shape((8, docs), i32)),
        2 * slots * docs * wide,
        docs * width * 4 + slots * wide * 2,
        in_specs=[pl.BlockSpec(memory_space=pltpu.HBM)] * 3,
        scratch_shapes=[
            pltpu.VMEM((docs, width), f32),
            pltpu.VMEM((2, 1, docs), i32),
            pltpu.SemaphoreType.DMA((3,)),
        ],
    )(*(in_hbm(x) for x in (embeddings, cluster.reshape(1, docs), order.reshape(1, docs))))
    own = lax.all_to_all(packed, ("zy", "x"), split_axis=0, concat_axis=0, tiled=True)
    other = lax.ppermute(own, "core", [(0, 1), (1, 0)])
    flops = 2 * slots * slots * width
    queries, rank, first = call(
        own_kernel,
        (shape((width, slots), bf16), shape((8, slots), f32), shape((8, slots), f32)),
        flops,
        2 * slots * wide * 2,
    )(own)
    best = call(other_kernel, shape((CLUSTERS, LANES), f32), flops, 2 * slots * wide * 2)(
        other, queries, rank, first
    )
    back = lax.all_to_all(best, ("zy", "x"), split_axis=0, concat_axis=0, tiled=True)
    result = call(unpack_kernel, shape((1, docs), f32), 0, CLUSTERS * LANES * 4)(back, where)
    return result.reshape(docs)


def solution(mesh):
    devices = mesh.devices.reshape(-1, CORES, mesh.shape["narrow"])
    chips = Mesh(devices, ("zy", "core", "x"))
    axes = ("zy", "core", "x")
    return jax.shard_map(
        per_device,
        mesh=chips,
        in_specs=(P(axes, None), P(axes), P(axes)),
        out_specs=P(axes),
        check_vma=False,
    )
```

profile of v0, /device:TPU:0, one launch (start us, length us, event | category | flops | bytes accessed | tf_op | source)
XLA Modules:
  0.0 51.7 jit_solution(2445892827441774716)
XLA Ops:
  0.0 1.6 %shard_map.37 = (bf16[512,1152]{1,0:T(8,128)(2,1)S(1)}, s32[8,128]{1,0:T(8,128)S(1)}) custom-call(f32[128,1024]{1,0:T(8,128)} %rows_hbm.1, s32[1,128]{1,0:T(1,128)} %bitcast.14, s32[1,128]{1,0:T(1,128)} %bitcast.15), custom_call_target="tpu_custom_call" | custom-call | flops 150994944 | bytes 1703936 | tf_op jit(solution)/shard_map/pallas_call | solution.py:141
  1.6 31.6 %all_to_all.22 = bf16[64,8,1152]{2,1,0:T(8,128)(2,1)S(1)} all-to-all(bf16[64,8,1152]{2,1,0:T(8,128)(2,1)S(1)} %bitcast.11), channel_id=1, replica_groups=mesh['zy'=16,'core'=2,'x'=4] {'zy','x'}, dimensions={0} | all-to-all | bytes 2359296 | tf_op jit(solution)/shard_map/all_to_all | solution.py:153
  33.2 0.0 collective-permute-start
  33.2 0.8 %shard_map.38 = (bf16[1024,512]{1,0:T(8,128)(2,1)S(1)}, f32[8,512]{1,0:T(8,128)S(1)}, f32[8,512]{1,0:T(8,128)S(1)}) custom-call(bf16[512,1152]{1,0:T(8,128)(2,1)S(1)} %bitcast.10), custom_call_target="tpu_custom_call" | custom-call | flops 536870912 | bytes 2359296 | tf_op jit(solution)/shard_map/pallas_call | solution.py:156
  34.0 2.0 %collective-permute-done.other_ref = bf16[512,1152]{1,0:T(8,128)(2,1)S(1)} collective-permute-done((bf16[512,1152]{1,0:T(8,128)(2,1)S(1)}, bf16[512,1152]{1,0:T(8,128)(2,1)S(1)}, u32[]{:S(2)}, u32[]{:S(2)}) %collective-permute-start) | collective-permute-done | bytes 1179680 | tf_op jit(solution)/shard_map/ppermute | solution.py:154
  36.1 0.7 %shard_map.39 = f32[64,128]{1,0:T(8,128)S(1)} custom-call(bf16[512,1152]{1,0:T(8,128)(2,1)S(1)} %collective-permute-done.other_ref, bf16[1024,512]{1,0:T(8,128)(2,1)S(1)} %get-tuple-element.11.queries_ref, f32[8,512]{1,0:T(8,128)S(1)} %get-tuple-element.12.rank_ref, f32[8,512]{1,0:T(8,128)S(1)} %get-tuple-element.13.first_ref), custom_call_target="tpu_custom_call" | custom-call | flops 536870912 | bytes 2359296 | tf_op jit(solution)/shard_map/pallas_call | solution.py:162
  36.8 14.2 %all_to_all.23 = f32[64,1,128]{2,1,0:T(1,128)S(1)} all-to-all(f32[64,1,128]{2,1,0:T(1,128)S(1)} %bitcast.12), channel_id=1, replica_groups=mesh['zy'=16,'core'=2,'x'=4] {'zy','x'}, dimensions={0} | all-to-all | bytes 65536 | tf_op jit(solution)/shard_map/all_to_all | solution.py:165
  51.0 0.7 %shard_map.40 = f32[1,128]{1,0:T(1,128)} custom-call(f32[64,128]{1,0:T(8,128)S(1)} %bitcast.13, s32[8,128]{1,0:T(8,128)S(1)} %get-tuple-element.14.where_ref), custom_call_target="tpu_custom_call" | custom-call | bytes 32768 | tf_op jit(solution)/shard_map/pallas_call | solution.py:166
Async XLA Ops:
  33.2 2.8 %collective-permute-start = (bf16[512,1152]{1,0:T(8,128)(2,1)S(1)}, bf16[512,1152]{1,0:T(8,128)(2,1)S(1)}, u32[]{:S(2)}, u32[]{:S(2)}) collective-permute-start(bf16[512,1152]{1,0:T(8,128)(2,1)S(1)} %bitcast.9), channel_id=1, source_target_pairs={{0,4},{4,0},{1,5},{5,1},{2,6},{6,2},{3,7},{7,3},{8,12},{12,8},{9,1... | collective-permute-start | bytes 3538952 | tf_op jit(solution)/shard_map/ppermute | solution.py:154
where the time goes:
time: 51.9 us; the launch traced here: 51.7 us
  blocking collectives  45.8 us (88%)
  Pallas kernels  3.85 us (7%)
  waiting for transfers between devices  2.03 us (4%)
    all_to_all x1, blocking collectives, per_device(): lax.all_to_all(packed, ('zy', 'x'), split_axis=0, concat_axis=0, tiled=True)  31.6 us
    all_to_all x1, blocking collectives, per_device(): lax.all_to_all(best, ('zy', 'x'), split_axis=0, concat_axis=0, tiled=True)  14.2 us
    ppermute x1, waiting for transfers between devices, per_device(): other = lax.ppermute(own, 'core', [(0, 1), (1, 0)])  2.03 us
    pallas_call x1, Pallas kernels, per_device(): call(pack_kernel, (shape((slots, wide), bf16), shape((8, docs), i32)), 2...  1.62 us
  transfers between devices with their start and end apart: 1, of which 1 were waited for; matrix products, arithmetic and copies ran while one was open for 0% of the time, Pallas kernels for 2%

commit v1 on v0

v1 whole, which is shorter than its diff:
```python
import jax
import jax.numpy as jnp
from jax import lax
from jax.experimental import pallas as pl
from jax.experimental.pallas import tpu as pltpu
from jax.sharding import Mesh, PartitionSpec as P

CLUSTERS = 64
SLOTS = 8
CAP = 512
LANES = 128
CORES = 2
CHUNKS = 4
GROUPS = CLUSTERS // CHUNKS
PART = GROUPS * SLOTS
TILES = 33
epsilon = 1e-06

VMEM = 32 * 1024 * 1024
NT = (((1,), (1,)), ((), ()))


def iota(shape, axis):
    return lax.broadcasted_iota(jnp.int32, shape, axis)


def as_bf16(mask):
    return jnp.where(mask, 1.0, 0.0).astype(jnp.bfloat16)


def pack_kernel(rows_hbm, cluster_hbm, order_hbm, out_ref, where_ref, rows_ref, ids_ref, sems):
    docs, width = rows_ref.shape
    cluster_copy = pltpu.make_async_copy(cluster_hbm, ids_ref.at[0], sems.at[0])
    order_copy = pltpu.make_async_copy(order_hbm, ids_ref.at[1], sems.at[1])
    rows_copy = pltpu.make_async_copy(rows_hbm, rows_ref, sems.at[2])
    cluster_copy.start()
    order_copy.start()
    rows_copy.start()
    before = as_bf16(iota((docs, docs), 0) < iota((docs, docs), 1))
    cluster_copy.wait()
    order_copy.wait()
    cluster = ids_ref[0]
    member = iota((CLUSTERS, docs), 0) == cluster
    count = jnp.dot(as_bf16(member), before, preferred_element_type=jnp.float32)
    position = jnp.sum(jnp.where(member, count, 0.0), axis=0, keepdims=True).astype(jnp.int32)
    chip = lax.axis_index("zy") * lax.axis_size("x") + lax.axis_index("x")
    where_ref[0:1] = cluster
    where_ref[1:2] = chip // CHUNKS * SLOTS + (chip % CHUNKS * 2 + position) % SLOTS
    chunk = cluster % CHUNKS
    start = chunk * PART + cluster // CHUNKS * SLOTS
    line = iota((CHUNKS * PART, docs), 0)
    place = as_bf16(line == start + (chunk * 2 + position) % SLOTS)
    rank = ids_ref[1] - CAP
    high = (rank >> 4).astype(jnp.float32)
    low = (rank & 15).astype(jnp.float32)
    high_line = start + chunk * 2
    marks = jnp.where(line == high_line, high, jnp.where(line == high_line + 1, low, 0.0))
    marks = lax.dot_general(
        marks.astype(jnp.bfloat16),
        as_bf16(iota((LANES, docs), 0) == position),
        NT,
        preferred_element_type=jnp.float32,
    )
    rows_copy.wait()
    rows = rows_ref[...]
    squares = jnp.sum(rows * rows, axis=1, keepdims=True)
    unit = (rows * lax.rsqrt(squares + epsilon)).astype(jnp.bfloat16)
    slot = iota((GROUPS, SLOTS, LANES), 1)
    carried = None
    for at in range(CHUNKS):
        part = slice(at * PART, (at + 1) * PART)
        packed = jnp.dot(place[part], unit, preferred_element_type=jnp.float32)
        mine = slot >= at * 2
        for lane in range(0, width, LANES):
            tile = packed[:, lane : lane + LANES].reshape(GROUPS, SLOTS, LANES)
            value = tile if carried is None else jnp.where(mine, tile, carried)
            out_ref[:, at * 8 + lane // LANES] = value.astype(jnp.bfloat16)
            carried = tile
        mark = marks[part].reshape(GROUPS, SLOTS, LANES)
        carried = jnp.where(mine, mark, carried)
    out_ref[:, TILES - 1] = carried.astype(jnp.bfloat16)


def unfold(ref):
    slot = iota((GROUPS, SLOTS, LANES), 1)
    lane = iota((GROUPS, SLOTS, LANES), 2)
    rows, ranks = [], []
    for chunk in range(CHUNKS):
        turn = chunk * 2
        tiles = [ref[:, chunk * 8 + i] for i in range(9)]
        if chunk > 0:
            line = slot.astype(jnp.float32).astype(jnp.bfloat16)
            mine = line >= jnp.asarray(turn, jnp.bfloat16)
            data = [jnp.where(mine, x, y) for x, y in zip(tiles[:-1], tiles[1:])]
        else:
            data = tiles[:-1]
        rows.append(jnp.concatenate([x.reshape(PART, LANES) for x in data], axis=1))
        marks = tiles[-1].astype(jnp.float32)
        rank = marks[:, turn : turn + 1] * 16.0 + marks[:, turn + 1 : turn + 2]
        mine = lane == (slot - turn) % SLOTS
        rank = jnp.sum(jnp.where(mine, rank, 0.0), axis=2, keepdims=True)
        ranks.append(jnp.broadcast_to(rank, (GROUPS, SLOTS, LANES)).reshape(PART, LANES))
    return jnp.concatenate(rows, axis=0), jnp.concatenate(ranks, axis=0)


def best_of(keys, key_rank, queries_ref, rank_ref, first):
    step = 2 * LANES
    best = []
    for at in range(0, queries_ref.shape[1], step):
        similar = jnp.dot(
            keys, queries_ref[:, at : at + step], preferred_element_type=jnp.float32
        )
        for lane in range(0, step, LANES):
            allowed = key_rank < rank_ref[0:1, at + lane : at + lane + LANES]
            value = jnp.where(allowed, similar[:, lane : lane + LANES], -1.0)
            value = jnp.max(value.reshape(-1, 8, LANES), axis=0)
            best.append(jnp.maximum(value, first[:, at + lane : at + lane + LANES]))
    return best


def own_kernel(own_ref, queries_ref, rank_ref, best_ref):
    rows, ranks = unfold(own_ref)
    queries_ref[...] = rows.T
    rank_ref[...] = ranks.T[0:8]
    first = jnp.full(best_ref.shape, -1.0, jnp.float32)
    for at, best in enumerate(best_of(rows, ranks, queries_ref, rank_ref, first)):
        best_ref[:, at * LANES : (at + 1) * LANES] = best


def other_kernel(other_ref, queries_ref, rank_ref, first_ref, out_ref):
    rows, ranks = unfold(other_ref)
    best = best_of(rows, ranks, queries_ref, rank_ref, first_ref[...])
    lines = jnp.concatenate([jnp.max(x, axis=0, keepdims=True) for x in best])
    lines = jnp.concatenate([lines, lines])
    for at in range(0, CLUSTERS, 8):
        out_ref[at : at + 8] = lines


def unpack_kernel(best_ref, where_ref, out_ref):
    docs = where_ref.shape[1]
    best = jnp.concatenate([best_ref[...], jnp.zeros((LANES - CLUSTERS, LANES), jnp.float32)])
    cluster = jnp.broadcast_to(where_ref[0:1], (LANES, docs))
    by_cluster = jnp.take_along_axis(best.T, cluster, axis=1)
    wanted = iota((LANES, docs), 0) == where_ref[1:2]
    out_ref[...] = jnp.sum(jnp.where(wanted, by_cluster, 0.0), axis=0, keepdims=True)


def call(kernel, out_shape, flops, moved, **more):
    return pl.pallas_call(
        kernel,
        out_shape=out_shape,
        compiler_params=pltpu.CompilerParams(vmem_limit_bytes=VMEM),
        cost_estimate=pl.CostEstimate(flops=flops, bytes_accessed=moved, transcendentals=0),
        **more,
    )


def in_hbm(x):
    return pltpu.with_memory_space_constraint(x, pltpu.HBM)


def per_device(embeddings, cluster, order):
    docs, width = embeddings.shape
    slots = CLUSTERS * SLOTS
    shape = jax.ShapeDtypeStruct
    f32, bf16, i32 = jnp.float32, jnp.bfloat16, jnp.int32
    tiles = (GROUPS, TILES, 8, LANES)
    moved = CLUSTERS * (SLOTS * width + 2 * LANES) * 2
    packed, where = call(
        pack_kernel,
        (shape(tiles, bf16), shape((8, docs), i32)),
        2 * slots * docs * width,
        docs * width * 4 + moved,
        in_specs=[pl.BlockSpec(memory_space=pltpu.HBM)] * 3,
        scratch_shapes=[
            pltpu.VMEM((docs, width), f32),
            pltpu.VMEM((2, 1, docs), i32),
            pltpu.SemaphoreType.DMA((3,)),
        ],
    )(*(in_hbm(x) for x in (embeddings, cluster.reshape(1, docs), order.reshape(1, docs))))
    chunks = packed.reshape(CLUSTERS, TILES, 2, LANES)
    own = lax.all_to_all(chunks, ("zy", "x"), split_axis=0, concat_axis=0, tiled=True)
    other = lax.ppermute(own, "core", [(0, 1), (1, 0)])
    flops = 2 * slots * slots * width
    queries, rank, first = call(
        own_kernel,
        (shape((width, slots), bf16), shape((8, slots), f32), shape((8, slots), f32)),
        flops,
        2 * moved,
    )(own.reshape(tiles))
    best = call(other_kernel, shape((CLUSTERS, LANES), f32), flops, 2 * moved)(
        other.reshape(tiles), queries, rank, first
    )
    back = lax.all_to_all(best, ("zy", "x"), split_axis=0, concat_axis=0, tiled=True)
    result = call(unpack_kernel, shape((1, docs), f32), 0, CLUSTERS * LANES * 4)(back, where)
    return result.reshape(docs)


def solution(mesh):
    devices = mesh.devices.reshape(-1, CORES, mesh.shape["narrow"])
    chips = Mesh(devices, ("zy", "core", "x"))
    axes = ("zy", "core", "x")
    return jax.shard_map(
        per_device,
        mesh=chips,
        in_specs=(P(axes, None), P(axes), P(axes)),
        out_specs=P(axes),
        check_vma=False,
    )
```

time: 51.9 us -> 50.6 us (0.975)
  blocking collectives: 45.8 us -> 44.6 us
    all_to_all x1, blocking collectives: 31.6 us -> 30.5 us  [per_device(): lax.all_to_all(chunks, ('zy', 'x'), split_axis=0, concat_axis=0, tiled=True)]
where the time goes in v1:
time: 50.6 us; the launch traced here: 50.4 us
  blocking collectives  44.6 us (88%)
  Pallas kernels  3.87 us (8%)
  waiting for transfers between devices  1.9 us (4%)
    all_to_all x1, blocking collectives, per_device(): lax.all_to_all(chunks, ('zy', 'x'), split_axis=0, concat_axis=0, tiled=True)  30.5 us
    all_to_all x1, blocking collectives, per_device(): lax.all_to_all(best, ('zy', 'x'), split_axis=0, concat_axis=0, tiled=True)  14.1 us
    ppermute x1, waiting for transfers between devices, per_device(): other = lax.ppermute(own, 'core', [(0, 1), (1, 0)])  1.9 us
    pallas_call x1, Pallas kernels, per_device(): call(pack_kernel, (shape(tiles, bf16), shape((8, docs), i32)), 2 * slots...  1.66 us
  transfers between devices with their start and end apart: 1, of which 1 were waited for; matrix products, arithmetic and copies ran while one was open for 0% of the time, Pallas kernels for 2%

profile of v1, /device:TPU:0, one launch (start us, length us, event | category | flops | bytes accessed | tf_op | source)
XLA Modules:
  0.0 50.4 jit_solution(11846325673532318130)
XLA Ops:
  0.0 1.7 %shard_map.37 = (bf16[16,33,8,128]{3,2,1,0:T(8,128)(2,1)S(1)}, s32[8,128]{1,0:T(8,128)S(1)}) custom-call(f32[128,1024]{1,0:T(8,128)} %rows_hbm.1, s32[1,128]{1,0:T(1,128)} %bitcast.15, s32[1,128]{1,0:T(1,128)} %bitcast.16), custom_call_target="tpu_custom_call" | custom-call | flops 134217728 | bytes 1605632 | tf_op jit(solution)/shard_map/pallas_call | solution.py:169
  1.7 30.5 %all_to_all.16 = bf16[64,33,2,128]{3,2,1,0:T(2,128)(2,1)S(1)} all-to-all(bf16[64,33,2,128]{3,2,1,0:T(2,128)(2,1)S(1)} %bitcast.12), channel_id=1, replica_groups=mesh['zy'=16,'core'=2,'x'=4] {'zy','x'}, dimensions={0} | all-to-all | bytes 2162688 | tf_op jit(solution)/shard_map/all_to_all | solution.py:182
  32.2 0.0 collective-permute-start
  32.2 0.8 %shard_map.38 = (bf16[1024,512]{1,0:T(8,128)(2,1)S(1)}, f32[8,512]{1,0:T(8,128)S(1)}, f32[8,512]{1,0:T(8,128)S(1)}) custom-call(bf16[16,33,8,128]{3,2,1,0:T(8,128)(2,1)S(1)} %bitcast.11), custom_call_target="tpu_custom_call" | custom-call | flops 536870912 | bytes 2162688 | tf_op jit(solution)/shard_map/pallas_call | solution.py:185
  33.0 1.9 %collective-permute-done = bf16[64,33,2,128]{3,2,1,0:T(2,128)(2,1)S(1)} collective-permute-done((bf16[64,33,2,128]{3,2,1,0:T(2,128)(2,1)S(1)}, bf16[64,33,2,128]{3,2,1,0:T(2,128)(2,1)S(1)}, u32[]{:S(2)}, u32[]{:S(2)}) %collective-permute-start) | collective-permute-done | bytes 1081376 | tf_op jit(solution)/shard_map/ppermute | solution.py:183
  34.9 0.7 %shard_map.39 = f32[64,128]{1,0:T(8,128)S(1)} custom-call(bf16[16,33,8,128]{3,2,1,0:T(8,128)(2,1)S(1)} %bitcast.10, bf16[1024,512]{1,0:T(8,128)(2,1)S(1)} %get-tuple-element.11.queries_ref, f32[8,512]{1,0:T(8,128)S(1)} %get-tuple-element.12.rank_ref, f32[8,512]{1,0:T(8,128)S(1)} %get-tuple-element.13.first_ref), custom_call_target="tpu_custom_call" | custom-call | flops 536870912 | bytes 2162688 | tf_op jit(solution)/shard_map/pallas_call | solution.py:191
  35.6 14.1 %all_to_all.17 = f32[64,1,128]{2,1,0:T(1,128)S(1)} all-to-all(f32[64,1,128]{2,1,0:T(1,128)S(1)} %bitcast.13), channel_id=1, replica_groups=mesh['zy'=16,'core'=2,'x'=4] {'zy','x'}, dimensions={0} | all-to-all | bytes 65536 | tf_op jit(solution)/shard_map/all_to_all | solution.py:194
  49.7 0.7 %shard_map.40 = f32[1,128]{1,0:T(1,128)} custom-call(f32[64,128]{1,0:T(8,128)S(1)} %bitcast.14, s32[8,128]{1,0:T(8,128)S(1)} %get-tuple-element.14.where_ref), custom_call_target="tpu_custom_call" | custom-call | bytes 32768 | tf_op jit(solution)/shard_map/pallas_call | solution.py:195
Async XLA Ops:
  32.2 2.7 %collective-permute-start = (bf16[64,33,2,128]{3,2,1,0:T(2,128)(2,1)S(1)}, bf16[64,33,2,128]{3,2,1,0:T(2,128)(2,1)S(1)}, u32[]{:S(2)}, u32[]{:S(2)}) collective-permute-start(bf16[64,33,2,128]{3,2,1,0:T(2,128)(2,1)S(1)} %all_to_all.16), channel_id=1, source_target_pairs={{0,4},{4,0},{1,5},{5,1},{2,6},{6,2},{3,7},{7,3},{8,12},{12,8},{9,1... | collective-permute-start | bytes 3244040 | tf_op jit(solution)/shard_map/ppermute | solution.py:183

commit v2 on v1

--- a/solution.py
+++ b/solution.py
@@ -43,7 +43,7 @@
     member = iota((CLUSTERS, docs), 0) == cluster
     count = jnp.dot(as_bf16(member), before, preferred_element_type=jnp.float32)
     position = jnp.sum(jnp.where(member, count, 0.0), axis=0, keepdims=True).astype(jnp.int32)
-    chip = lax.axis_index("zy") * lax.axis_size("x") + lax.axis_index("x")
+    chip = lax.axis_index("x") * lax.axis_size("zy") + lax.axis_index("zy")
     where_ref[0:1] = cluster
     where_ref[1:2] = chip // CHUNKS * SLOTS + (chip % CHUNKS * 2 + position) % SLOTS
     chunk = cluster % CHUNKS
@@ -65,20 +65,21 @@
     rows = rows_ref[...]
     squares = jnp.sum(rows * rows, axis=1, keepdims=True)
     unit = (rows * lax.rsqrt(squares + epsilon)).astype(jnp.bfloat16)
-    slot = iota((GROUPS, SLOTS, LANES), 1)
+    line = iota((GROUPS, SLOTS, LANES), 1).astype(jnp.float32).astype(jnp.bfloat16)
     carried = None
     for at in range(CHUNKS):
         part = slice(at * PART, (at + 1) * PART)
         packed = jnp.dot(place[part], unit, preferred_element_type=jnp.float32)
-        mine = slot >= at * 2
+        packed = packed.astype(jnp.bfloat16)
+        mine = line >= jnp.asarray(at * 2, jnp.bfloat16)
         for lane in range(0, width, LANES):
             tile = packed[:, lane : lane + LANES].reshape(GROUPS, SLOTS, LANES)
             value = tile if carried is None else jnp.where(mine, tile, carried)
-            out_ref[:, at * 8 + lane // LANES] = value.astype(jnp.bfloat16)
+            out_ref[:, at * 8 + lane // LANES] = value
             carried = tile
-        mark = marks[part].reshape(GROUPS, SLOTS, LANES)
+        mark = marks[part].astype(jnp.bfloat16).reshape(GROUPS, SLOTS, LANES)
         carried = jnp.where(mine, mark, carried)
-    out_ref[:, TILES - 1] = carried.astype(jnp.bfloat16)
+    out_ref[:, TILES - 1] = carried
 
 
 def unfold(ref):
@@ -179,7 +180,7 @@
         ],
     )(*(in_hbm(x) for x in (embeddings, cluster.reshape(1, docs), order.reshape(1, docs))))
     chunks = packed.reshape(CLUSTERS, TILES, 2, LANES)
-    own = lax.all_to_all(chunks, ("zy", "x"), split_axis=0, concat_axis=0, tiled=True)
+    own = lax.all_to_all(chunks, ("x", "zy"), split_axis=0, concat_axis=0, tiled=True)
     other = lax.ppermute(own, "core", [(0, 1), (1, 0)])
     flops = 2 * slots * slots * width
     queries, rank, first = call(
@@ -191,7 +192,7 @@
     best = call(other_kernel, shape((CLUSTERS, LANES), f32), flops, 2 * moved)(
         other.reshape(tiles), queries, rank, first
     )
-    back = lax.all_to_all(best, ("zy", "x"), split_axis=0, concat_axis=0, tiled=True)
+    back = lax.all_to_all(best, ("x", "zy"), split_axis=0, concat_axis=0, tiled=True)
     result = call(unpack_kernel, shape((1, docs), f32), 0, CLUSTERS * LANES * 4)(back, where)
     return result.reshape(docs)
 

time: 50.6 us -> 50.4 us (level)
  no operation moved by 1% of the time
where the time goes in v2:
time: 50.4 us; the launch traced here: 50.2 us
  blocking collectives  44.4 us (88%)
  Pallas kernels  3.87 us (8%)
  waiting for transfers between devices  1.9 us (4%)
    all_to_all x1, blocking collectives, per_device(): lax.all_to_all(chunks, ('x', 'zy'), split_axis=0, concat_axis=0, tiled=True)  30.2 us
    all_to_all x1, blocking collectives, per_device(): lax.all_to_all(best, ('x', 'zy'), split_axis=0, concat_axis=0, tiled=True)  14.2 us
    ppermute x1, waiting for transfers between devices, per_device(): other = lax.ppermute(own, 'core', [(0, 1), (1, 0)])  1.9 us
    pallas_call x1, Pallas kernels, per_device(): call(pack_kernel, (shape(tiles, bf16), shape((8, docs), i32)), 2 * slots...  1.66 us
  transfers between devices with their start and end apart: 1, of which 1 were waited for; matrix products, arithmetic and copies ran while one was open for 0% of the time, Pallas kernels for 2%

profile of v2, /device:TPU:0, one launch (start us, length us, event | category | flops | bytes accessed | tf_op | source)
XLA Modules:
  0.0 50.2 jit_solution(805931336643786974)
XLA Ops:
  0.0 1.7 %shard_map.37 = (bf16[16,33,8,128]{3,2,1,0:T(8,128)(2,1)S(1)}, s32[8,128]{1,0:T(8,128)S(1)}) custom-call(f32[128,1024]{1,0:T(8,128)} %rows_hbm.1, s32[1,128]{1,0:T(1,128)} %bitcast.15, s32[1,128]{1,0:T(1,128)} %bitcast.16), custom_call_target="tpu_custom_call" | custom-call | flops 134217728 | bytes 1605632 | tf_op jit(solution)/shard_map/pallas_call | solution.py:170
  1.7 30.2 %all_to_all.16 = bf16[64,33,2,128]{3,2,1,0:T(2,128)(2,1)S(1)} all-to-all(bf16[64,33,2,128]{3,2,1,0:T(2,128)(2,1)S(1)} %bitcast.12), channel_id=1, replica_groups=mesh['zy'=16,'core'=2,'x'=4] {'x','zy'}, dimensions={0} | all-to-all | bytes 2162688 | tf_op jit(solution)/shard_map/all_to_all | solution.py:183
  31.8 0.0 collective-permute-start
  31.9 0.8 %shard_map.38 = (bf16[1024,512]{1,0:T(8,128)(2,1)S(1)}, f32[8,512]{1,0:T(8,128)S(1)}, f32[8,512]{1,0:T(8,128)S(1)}) custom-call(bf16[16,33,8,128]{3,2,1,0:T(8,128)(2,1)S(1)} %bitcast.11), custom_call_target="tpu_custom_call" | custom-call | flops 536870912 | bytes 2162688 | tf_op jit(solution)/shard_map/pallas_call | solution.py:186
  32.7 1.9 %collective-permute-done = bf16[64,33,2,128]{3,2,1,0:T(2,128)(2,1)S(1)} collective-permute-done((bf16[64,33,2,128]{3,2,1,0:T(2,128)(2,1)S(1)}, bf16[64,33,2,128]{3,2,1,0:T(2,128)(2,1)S(1)}, u32[]{:S(2)}, u32[]{:S(2)}) %collective-permute-start) | collective-permute-done | bytes 1081376 | tf_op jit(solution)/shard_map/ppermute | solution.py:184
  34.6 0.7 %shard_map.39 = f32[64,128]{1,0:T(8,128)S(1)} custom-call(bf16[16,33,8,128]{3,2,1,0:T(8,128)(2,1)S(1)} %bitcast.10, bf16[1024,512]{1,0:T(8,128)(2,1)S(1)} %get-tuple-element.11.queries_ref, f32[8,512]{1,0:T(8,128)S(1)} %get-tuple-element.12.rank_ref, f32[8,512]{1,0:T(8,128)S(1)} %get-tuple-element.13.first_ref), custom_call_target="tpu_custom_call" | custom-call | flops 536870912 | bytes 2162688 | tf_op jit(solution)/shard_map/pallas_call | solution.py:192
  35.3 14.2 %all_to_all.17 = f32[64,1,128]{2,1,0:T(1,128)S(1)} all-to-all(f32[64,1,128]{2,1,0:T(1,128)S(1)} %bitcast.13), channel_id=1, replica_groups=mesh['zy'=16,'core'=2,'x'=4] {'x','zy'}, dimensions={0} | all-to-all | bytes 65536 | tf_op jit(solution)/shard_map/all_to_all | solution.py:195
  49.5 0.7 %shard_map.40 = f32[1,128]{1,0:T(1,128)} custom-call(f32[64,128]{1,0:T(8,128)S(1)} %bitcast.14, s32[8,128]{1,0:T(8,128)S(1)} %get-tuple-element.14.where_ref), custom_call_target="tpu_custom_call" | custom-call | bytes 32768 | tf_op jit(solution)/shard_map/pallas_call | solution.py:196
Async XLA Ops:
  31.8 2.7 %collective-permute-start = (bf16[64,33,2,128]{3,2,1,0:T(2,128)(2,1)S(1)}, bf16[64,33,2,128]{3,2,1,0:T(2,128)(2,1)S(1)}, u32[]{:S(2)}, u32[]{:S(2)}) collective-permute-start(bf16[64,33,2,128]{3,2,1,0:T(2,128)(2,1)S(1)} %all_to_all.16), channel_id=1, source_target_pairs={{0,4},{4,0},{1,5},{5,1},{2,6},{6,2},{3,7},{7,3},{8,12},{12,8},{9,1... | collective-permute-start | bytes 3244040 | tf_op jit(solution)/shard_map/ppermute | solution.py:184
